TPU v7x, 32 devices: a whole 2x2x4 slice. The times are simulated.
32 devices in a mesh: wave: 8 (over z, y), lev: 4 (over x, core).
Axes of the slice: x: 2, y: 2, z: 4, core: 2. Of those that a mesh axis runs over, the one named last changes fastest.
Arguments:
- fourier: float32 [2560, 6, 1088], P('wave', None, 'lev'), may hold values from -6 to 6
- weights: float32 [2560], P('wave'), may hold values from 0.3 to 3
- row_points: int32 [2560], replicated, may hold values from 20 to 5164, as said below
- slot_map: int32 [6], replicated, may hold values from 0 to 7, as said below
- legendre_lookup: float32 [8, 2, 640, 1280], P('wave'), may hold values from -0.15625 to 0.15625
- to_modes: float32 [136, 136], replicated, may hold values from -0.5 to 0.5
- from_modes: float32 [136, 136], replicated, may hold values from -0.5 to 0.5
- mode_rates: float32 [136], replicated, may hold values from 0.1 to 10
- thermal_response_matrix: float32 [136, 136], replicated, may hold values from -0.5 to 0.5
Outputs:
- spectra: float32 [8, 2, 640, 1088], P('wave', None, 'lev')
Inputs may be any that keep to these rules, and one draw needn't show every extreme that they name: `row_points`: row t has 20 + 4 * d + 4 * q points, d its distance in rows from the nearer pole and q a whole number from 0 to 7; row 1279, the last row of the northern hemisphere, reaches the largest value. `slot_map`: distinct global slots; slot s is held by device s of wave (one slot per device); which slots, and so which devices, hold a wavenumber is drawn from the seed.
All inputs are finite; a program needn't handle non-finite values.
Results may differ from a plain program's by a relative error of at most 0.0003.
Values sent between devices are 32-bit elements; how exact they have to be, the bound alone decides.
A program may use at most 64 MiB of HBM per device.

v0:
```python
import jax
import jax.numpy as jnp
from jax import lax
from jax.sharding import PartitionSpec as P

NTRUNC = 1280
LEVELS = 136
FIELDS = 4


def vertical_step(spectra, degree, to_modes, from_modes, mode_rates, thermal_response_matrix):
    maximal_wave_truncation = lax.Precision.HIGHEST
    layerwise_coefficients = spectra.reshape(spectra.shape[:-1] + (LEVELS, FIELDS, 2))
    divergence = layerwise_coefficients[..., 1, :]
    modal = jnp.einsum("kl,...lc->...kc", to_modes, divergence, precision=maximal_wave_truncation)
    degrees = degree.astype(jnp.float32)
    wave_ratio = degrees * (degrees + 1.0) / (NTRUNC * NTRUNC)
    damping = 1.0 / (1.0 + mode_rates * wave_ratio[..., None])
    advanced_flow_spreading = jnp.einsum(
        "mc,...cb->...mb", from_modes, modal * damping[..., None], precision=maximal_wave_truncation
    )
    advanced_thermal_field = layerwise_coefficients[..., 2, :] - jnp.einsum(
        "mc,...cb->...mb",
        thermal_response_matrix,
        advanced_flow_spreading,
        precision=maximal_wave_truncation,
    )
    joined_coefficient_sets = jnp.stack(
        [
            layerwise_coefficients[..., 0, :],
            advanced_flow_spreading,
            advanced_thermal_field,
            layerwise_coefficients[..., 3, :],
        ],
        axis=-2,
    )
    return joined_coefficient_sets.reshape(spectra.shape)


def legendre_sums(paired, tables):
    maximal_wave_truncation = lax.Precision.HIGHEST
    return jnp.einsum("spih,phsc->spic", tables, paired, precision=maximal_wave_truncation)


def on_device(
    fourier,
    weights,
    row_points,
    slot_map,
    legendre_lookup,
    to_modes,
    from_modes,
    mode_rates,
    thermal_response_matrix,
):
    wave_count = lax.axis_size("wave")
    layer_number = lax.axis_size("lev")
    wave_index = lax.axis_index("wave")
    level_index = lax.axis_index("lev")
    lat_local = fourier.shape[0]
    window = fourier.shape[1]
    columns = fourier.shape[2]
    slot_count = legendre_lookup.shape[0]
    half_rows = legendre_lookup.shape[2]
    lat_half = legendre_lookup.shape[3]
    all_slots = slot_count * wave_count
    lat_total = 2 * lat_half
    stride = NTRUNC // window
    wavenum = jnp.arange(window, dtype=jnp.int32) * stride
    points_here = lax.dynamic_slice_in_dim(row_points, wave_index * lat_local, lat_local, 0)
    retained = (2 * wavenum[None, :] < points_here[:, None]).astype(jnp.float32)
    weighted = fourier * (weights[:, None] * retained)[:, :, None]
    slot_ids = jnp.arange(all_slots, dtype=jnp.int32)
    matches = (slot_map[None, :] == slot_ids[:, None]).astype(jnp.int32)
    used_all = jnp.sum(matches, axis=1)
    source_all = jnp.sum(matches * jnp.arange(window, dtype=jnp.int32)[None, :], axis=1)
    outgoing = jnp.take(weighted, source_all, axis=1) * used_all.astype(jnp.float32)[None, :, None]
    outgoing = outgoing.reshape(lat_local, wave_count, slot_count, columns)
    arrived = lax.all_to_all(outgoing, "wave", split_axis=1, concat_axis=0, tiled=True)
    arrived = arrived.reshape(lat_total, slot_count, columns)
    northern = arrived[:lat_half]
    southern = arrived[lat_half:][::-1]
    paired = jnp.stack([northern + southern, northern - southern])
    owned_orders = lax.dynamic_slice_in_dim(source_all, wave_index * slot_count, slot_count, 0)
    degree_base = owned_orders * stride
    row_count = half_rows // layer_number
    row_start = level_index * row_count
    local_spectra = legendre_sums(paired, legendre_lookup)
    spectra = lax.all_to_all(local_spectra, "lev", split_axis=2, concat_axis=3, tiled=True)
    row_ids = row_start + jnp.arange(row_count, dtype=jnp.int32)
    parities = jnp.arange(2, dtype=jnp.int32)
    degree = degree_base[:, None, None] + 2 * row_ids[None, None, :] + parities[None, :, None]
    validity = (degree < NTRUNC).astype(jnp.float32)
    joined_coefficient_sets = vertical_step(
        spectra, degree, to_modes, from_modes, mode_rates, thermal_response_matrix
    )
    return joined_coefficient_sets * validity[..., None]


def solution(mesh):
    placed = (
        P("wave", None, "lev"),
        P("wave"),
        P(),
        P(),
        P("wave", None, None, None),
        P(),
        P(),
        P(),
        P(),
    )
    return jax.shard_map(
        on_device,
        mesh=mesh,
        in_specs=placed,
        out_specs=P("wave", None, "lev", None),
        check_vma=False,
    )
```

profile of v0, /device:TPU:0, one launch (start us, length us, event | category | flops | bytes accessed | tf_op | source)
XLA Modules:
  0.0 170.2 jit_solution(6794839391210299669)
XLA Ops:
  0.0 0.8 convert_reduce_fusion
  0.9 0.8 dynamic_slice.6
  1.7 0.8 compare_select_fusion
  2.4 1.9 %broadcast_multiply_fusion = f32[320,6,272]{0,2,1:T(8,128)S(1)} fusion(f32[320,6,272]{0,2,1:T(8,128)} %param.9, f32[320,6]{0,1:T(8,128)S(1)} %compare_select_fusion), kind=kLoop, calls=%fused_computation.12 | loop fusion | flops 522240 | bytes 4185600 | tf_op jit(solution)/shard_map/mul | solution.py:72
  4.3 2.5 %gather_fusion = f32[8,320,272]{1,2,0:T(8,128)} fusion(f32[320,6,272]{0,2,1:T(8,128)S(1)} %broadcast_multiply_fusion, s32[1024]{0:T(1024)S(1)} %pad_clamp_fusion), kind=kCustom, calls=%fused_computation | custom fusion | bytes 5570592 | tf_op jit(solution)/shard_map/jit(_take)/gather | solution.py:77
  6.8 2.2 %fusion.2 = f32[320,8,1,272]{0,3,2,1:T(8,128)S(1)} fusion(f32[8,320,272]{1,2,0:T(8,128)} %gather_fusion, f32[8]{0:T(128)S(1)} %convert_element_type.30, pred[8]{0:T(512)(128)(4,1)S(1)} %compare_and_fusion), kind=kLoop, calls=%fused_computation.4 | loop fusion | flops 1392640 | bytes 5570600 | tf_op jit(solution)/shard_map/mul | solution.py:77
  9.0 82.1 %all_to_all.30 = f32[320,8,1,272]{0,3,2,1:T(8,128)S(1)} all-to-all(f32[320,8,1,272]{0,3,2,1:T(8,128)S(1)} %fusion.2), channel_id=1, replica_groups=mesh['wave'=8,'lev'=4] {'wave'}, dimensions={1} | all-to-all | bytes 5570560 | tf_op jit(solution)/shard_map/all_to_all | solution.py:79
  91.1 0.2 fusion.20
  91.3 0.6 copy.36
  92.0 2.1 %slice.27 = f32[1280,1,272]{0,2,1:T(8,128)} reshape(f32[4,320,1,1,272]{1,0,4,3,2:T(4,128)S(1)} %copy.36) | data formatting | bytes 2785280 | tf_op jit(solution)/shard_map/slice | solution.py:82
  94.1 15.9 %rev.3 = f32[1280,1,272]{0,2,1:T(8,128)} reverse(f32[1280,1,272]{0,2,1:T(8,128)} %slice.27), dimensions={0} | reverse | bytes 2785280 | tf_op jit(solution)/shard_map/rev | solution.py:82
  110.0 0.6 copy.35
  110.7 2.1 %slice.25 = f32[1280,1,272]{0,2,1:T(8,128)} reshape(f32[4,320,1,1,272]{1,0,4,3,2:T(4,128)S(1)} %copy.35) | data formatting | bytes 2785280 | tf_op jit(solution)/shard_map/slice | solution.py:81
  112.7 1.7 add_bitcast_fusion
  114.4 9.2 %fusion.5 = f32[1,2,640,272]{2,3,1,0:T(8,128)S(1)} fusion(f32[1,2,640,1280]{3,2,1,0:T(8,128)} %param.13, f32[1,1280,1,272]{1,3,0,2:T(8,128)S(1)} %get-tuple-element.10, f32[1,1280,1,272]{1,3,0,2:T(8,128)S(1)} %get-tuple-element.9), kind=kOutput, calls=%fused_computation.9 | convolution fusion | flops 5348433920 | bytes 10731520 | tf_op jit(solution)/shard_map/spih,phsc->spic/dot_general | solution.py:42
  123.7 2.9 %copy.38 = f32[1,2,640,272]{3,1,0,2:T(2,128)} copy(f32[1,2,640,272]{2,3,1,0:T(8,128)S(1)} %fusion.5) | data formatting | bytes 2785280 | tf_op jit(solution)/shard_map/spih,phsc->spic/dot_general | solution.py:42
  126.5 3.9 %all-to-all-start.1 = ((f32[1,2,640,272]{3,1,0,2:T(2,128)}), f32[1,2,640,272]{3,1,0,2:T(2,128)S(1)}, u32[]{:S(2)}, u32[]{:S(2)}) async-start(f32[1,2,640,272]{3,1,0,2:T(2,128)} %copy.38), calls=%async_computation.1 | async-start | bytes 3932160 | tf_op jit(solution)/shard_map/all_to_all | solution.py:89
  130.5 0.6 dynamic_slice.7
  131.8 0.1 add_divide_fusion
  131.9 22.7 %all-to-all-done.1 = f32[1,2,640,272]{3,1,0,2:T(2,128)S(1)} async-done(((f32[1,2,640,272]{3,1,0,2:T(2,128)}), f32[1,2,640,272]{3,1,0,2:T(2,128)S(1)}, u32[]{:S(2)}, u32[]{:S(2)}) %all-to-all-start.1) | async-done | bytes 1392672 | tf_op jit(solution)/shard_map/all_to_all | solution.py:89
  154.5 1.3 copy-done.1
  155.9 4.4 %copy.50 = f32[1,2,4,160,272]{3,2,4,1,0:T(4,128)S(1)} copy(f32[1,2,4,160,272]{4,1,3,2,0:T(2,128)} %bitcast.102) | data formatting | bytes 2785280 | tf_op jit(solution)/shard_map/all_to_all | solution.py:89
  160.3 1.7 %copy.40 = f32[1,2,160,4,272]{2,1,4,3,0:T(2,128)S(1)} copy(f32[1,2,160,4,272]{2,3,4,1,0:T(4,128)S(1)} %bitcast.101) | data formatting | bytes 2785280 | tf_op jit(solution)/shard_map/all_to_all | solution.py:89
  162.0 0.8 fusion.21
  162.8 0.1 copy.51
  163.0 0.7 fusion.9
  163.8 0.6 fusion.14
  164.4 0.7 fusion.11
  165.2 0.1 pad_maximum_fusion
  165.3 1.7 %copy.45 = f32[1,2,160,136,4,2]{2,1,5,4,3,0:T(2,128)S(1)} copy(f32[1,2,160,136,4,2]{2,3,5,1,4,0:T(8,128)S(1)} %pad_maximum_fusion) | data formatting | bytes 2785280 | tf_op jit(solution)/shard_map/stack | solution.py:28
  167.0 0.1 broadcast_multiply_fusion.1
  167.2 3.0 %copy.46 = f32[1,2,160,1088]{3,2,1,0:T(8,128)} copy(f32[1,2,160,1088]{2,1,3,0:T(2,128)S(1)} %bitcast.100) | data formatting | bytes 2785280 | tf_op jit(solution)/shard_map/mul | solution.py:97
  (21 shorter events, 0.2 us)
Async XLA Ops:
  0.0 163.0 %copy-start = (f32[136,136]{1,0:T(8,128)S(1)}, f32[136,136]{1,0:T(8,128)}, u32[]{:S(2)}) copy-start(f32[136,136]{1,0:T(8,128)} %param.14) | copy-start | bytes 221956
  110.7 2.1 %copy-start.2 = (f32[1280,1,272]{0,2,1:T(8,128)S(1)}, f32[1280,1,272]{0,2,1:T(8,128)}, u32[]{:S(2)}) copy-start(f32[1280,1,272]{0,2,1:T(8,128)} %rev.3) | copy-start | bytes 4177924
  126.5 5.2 %copy-start.5 = (f32[136]{0:T(256)S(1)}, f32[136]{0:T(256)}, u32[]{:S(2)}) copy-start(f32[136]{0:T(256)} %param.16) | copy-start | bytes 1636
  126.5 28.0 %all-to-all-start.1 = ((f32[1,2,640,272]{3,1,0,2:T(2,128)}), f32[1,2,640,272]{3,1,0,2:T(2,128)S(1)}, u32[]{:S(2)}, u32[]{:S(2)}) async-start(f32[1,2,640,272]{3,1,0,2:T(2,128)} %copy.38), calls=%async_computation.1 | async-start | bytes 3932160 | tf_op jit(solution)/shard_map/all_to_all | solution.py:89
  154.5 1.3 copy-start.1
  162.8 1.0 copy-start.3
  162.9 1.5 copy-start.4
where the time goes:
time: 172 us; the launch traced here: 170 us
  blocking collectives  82.1 us (48%)
  local copies, waits for them, and re-layouts  41.5 us (24%)
  waiting for transfers between devices  22.7 us (13%)
  matrix products  11.3 us (7%)
  other arithmetic  7.83 us (5%)
  starting transfers between devices  3.91 us (2%)
    all_to_all x1, blocking collectives, on_device(): lax.all_to_all(outgoing, 'wave', split_axis=1, concat_axis=0, tiled=True)  82.1 us
    all_to_all x1, waiting for transfers between devices, on_device(): lax.all_to_all(local_spectra, 'lev', split_axis=2, concat_axis=3, tiled=T...  22.7 us
    rev x1, local copies, waits for them, and re-layouts, on_device(): southern = arrived[lat_half:][::-1]  15.9 us
    dot_general x1, matrix products, legendre_sums(): jnp.einsum('spih,phsc->spic', tables, paired, precision=maximal_wave_trun...  9.23 us
    all_to_all x2, local copies, waits for them, and re-layouts, on_device(): lax.all_to_all(local_spectra, 'lev', split_axis=2, concat_axis=3, tiled=T...  6.12 us
    all_to_all x1, starting transfers between devices, on_device(): lax.all_to_all(local_spectra, 'lev', split_axis=2, concat_axis=3, tiled=T...  3.91 us
  transfers between devices with their start and end apart: 1, of which 1 were waited for; matrix products, arithmetic and copies ran while one was open for 0% of the time, Pallas kernels for 0%

commit v1 on v0

--- a/solution.py
+++ b/solution.py
@@ -1,6 +1,9 @@
+import functools
 import jax
 import jax.numpy as jnp
 from jax import lax
+from jax.experimental import pallas as pl
+from jax.experimental.pallas import tpu as pltpu
 from jax.sharding import PartitionSpec as P
 
 NTRUNC = 1280
@@ -42,7 +45,7 @@
     return jnp.einsum("spih,phsc->spic", tables, paired, precision=maximal_wave_truncation)
 
 
-def on_device(
+def on_device_plain(
     fourier,
     weights,
     row_points,
@@ -97,6 +100,421 @@
     return joined_coefficient_sets * validity[..., None]
 
 
+F32 = jnp.float32
+BF16 = jnp.bfloat16
+HALF_TILE = 64
+LANES = 128
+LAST = 128
+MESH_IDS = pl.DeviceIdType.MESH
+
+
+def split(x):
+    high = x.astype(BF16)
+    return high, (x - high.astype(F32)).astype(BF16)
+
+
+def dot_nn(a, b):
+    return lax.dot_general(a, b, (((1,), (0,)), ((), ())), preferred_element_type=F32)
+
+
+def dot_nt(a, b):
+    return lax.dot_general(a, b, (((1,), (1,)), ((), ())), preferred_element_type=F32)
+
+
+def iota(shape, dim):
+    return lax.broadcasted_iota(jnp.int32, shape, dim)
+
+
+def one_hot(cond):
+    return cond.astype(F32).astype(BF16)
+
+
+def kernel(
+    sizes,
+    slot_map,
+    weights,
+    points,
+    fourier,
+    table_hbm,
+    to_modes,
+    from_modes,
+    rates,
+    thermal,
+    out,
+    table,
+    table_hi,
+    table_lo,
+    outgoing,
+    arrived,
+    pair_hi,
+    pair_lo,
+    spec_a,
+    spec_b,
+    got_a,
+    got_b,
+    m_hi,
+    m_lo,
+    g_hi,
+    g_lo,
+    damp,
+    modal,
+    table_sem,
+    wave_send,
+    wave_recv,
+    lev_send,
+    lev_recv,
+):
+    wave_count, lev_count, chunks, wave_steps, lev_steps = sizes
+    window, cols, lats = fourier.shape
+    _, half_rows, lat_half = table_hbm.shape
+    levels = to_modes.shape[0]
+    all_cols = cols * lev_count
+    mode_cols = 2 * levels
+    rows = half_rows // lev_count
+    stride = NTRUNC // window
+    tiles = lats // LANES
+    half_waves = wave_count // 2
+    w = lax.axis_index("wave")
+    v = lax.axis_index("lev")
+
+    barrier = pltpu.get_barrier_semaphore()
+    for k in wave_steps:
+        pl.semaphore_signal(
+            barrier, inc=1, device_id={"wave": lax.rem(w + k, wave_count)}, device_id_type=MESH_IDS
+        )
+    for k in lev_steps:
+        pl.semaphore_signal(
+            barrier, inc=1, device_id={"lev": lax.rem(v + k, lev_count)}, device_id_type=MESH_IDS
+        )
+    table_copy = pltpu.make_async_copy(table_hbm, table, table_sem)
+    table_copy.start()
+
+    def slot_source(slot):
+        source = jnp.int32(0)
+        used = jnp.int32(0)
+        for j in range(window):
+            hit = slot_map[j] == slot
+            source = jnp.where(hit, j, source)
+            used = jnp.where(hit, 1, used)
+        return source, used
+
+    south = (w >= half_waves).astype(jnp.int32)
+    mirrored = w + south * (wave_count - 1 - 2 * w)
+    odd = lax.rem(mirrored, 2)
+    place = iota((lats, lats), 1) + odd * HALF_TILE
+    place = jnp.where(place >= lats, place - lats, place)
+    place = place + south * (lats - 1 - 2 * place)
+    arrange = one_hot(iota((lats, lats), 0) == place)
+    point_row = points[pl.ds(w, 1), :]
+    weight_row = weights[...]
+
+    def arranged(slot, first, width, write):
+        source, used = slot_source(slot)
+        keep = (2 * stride * source < point_row).astype(F32) * used.astype(F32)
+        block = fourier[source, first : first + width, :] * (weight_row * keep)
+        high, low = split(block)
+        moved = dot_nn(high, arrange) + dot_nn(low, arrange)
+        for t in range(tiles):
+            write(t * width, width, moved[:, t * LANES : (t + 1) * LANES])
+        left = moved[: width // 2, tiles * LANES :]
+        right = moved[width // 2 :, tiles * LANES :]
+        write(tiles * width, width // 2, jnp.concatenate([left, right], axis=1))
+
+    def wave_copy(c, k):
+        first, width, base, length = chunks[c]
+        return pltpu.make_async_remote_copy(
+            src_ref=outgoing.at[k - 1, pl.ds(base, length)],
+            dst_ref=arrived.at[w, pl.ds(base, length)],
+            send_sem=wave_send.at[c, k - 1],
+            recv_sem=wave_recv.at[c, k - 1],
+            device_id={"wave": lax.rem(w + k, wave_count)},
+            device_id_type=MESH_IDS,
+        )
+
+    pl.semaphore_wait(barrier, len(wave_steps) + len(lev_steps))
+    for c, (first, width, base, length) in enumerate(chunks):
+        for k in wave_steps:
+
+            def put(at, count, value, k=k, base=base):
+                outgoing[k - 1, base + at : base + at + count, :] = value
+
+            arranged(lax.rem(w + k, wave_count), first, width, put)
+            wave_copy(c, k).start()
+    for first, width, base, length in chunks:
+
+        def put_own(at, count, value, base=base):
+            arrived[w, base + at : base + at + count, :] = value
+
+        arranged(w, first, width, put_own)
+
+    table_copy.wait()
+    step_rows = 32
+
+    @pl.loop(0, half_rows // step_rows)
+    def _(r):
+        at = pl.ds(pl.multiple_of(r * step_rows, step_rows), step_rows)
+        for p in range(2):
+            high, low = split(table[p, at, :])
+            table_hi[p, at, :] = high
+            table_lo[p, at, :] = low
+
+    part_mask = (
+        lax.rem(iota((all_cols, mode_cols), 0), 2) == lax.rem(iota((all_cols, mode_cols), 1), 2)
+    ).astype(F32)
+    part_mask_t = (
+        lax.rem(iota((mode_cols, all_cols), 0), 2) == lax.rem(iota((mode_cols, all_cols), 1), 2)
+    ).astype(F32)
+    group = 2 * FIELDS
+    col_id = iota((all_cols, levels), 0)
+    take_level = one_hot(
+        (lax.div(col_id, group) == iota((all_cols, levels), 1))
+        & (lax.div(lax.rem(col_id, group), 2) == 1)
+    )
+    spread = one_hot(lax.div(iota((levels, mode_cols), 1), 2) == iota((levels, mode_cols), 0))
+    for piece, held in zip(split(to_modes[...]), (m_hi, m_lo)):
+        picked = dot_nt(take_level, piece).astype(BF16)
+        held[...] = (dot_nn(picked, spread) * part_mask).astype(BF16)
+
+    from_hi, from_lo = split(from_modes[...])
+    th_hi, th_lo = split(thermal[...])
+    response = -(dot_nn(th_hi, from_hi) + dot_nn(th_hi, from_lo) + dot_nn(th_lo, from_hi))
+    resp_hi, resp_lo = split(response)
+    spread_t = one_hot(lax.div(iota((mode_cols, levels), 0), 2) == iota((mode_cols, levels), 1))
+    lane_id = iota((levels, all_cols), 1)
+    same_level = lax.div(lane_id, group) == iota((levels, all_cols), 0)
+    field = lax.div(lax.rem(lane_id, group), 2)
+    put_div = one_hot(same_level & (field == 1))
+    put_temp = one_hot(same_level & (field == 2))
+    for div_piece, temp_piece, held in ((from_hi, resp_hi, g_hi), (from_lo, resp_lo, g_lo)):
+        div_cols = dot_nt(spread_t, div_piece).astype(BF16)
+        temp_cols = dot_nt(spread_t, temp_piece).astype(BF16)
+        both = dot_nn(div_cols, put_div) + dot_nn(temp_cols, put_temp)
+        held[...] = (both * part_mask_t).astype(BF16)
+
+    own_source, _ = slot_source(w)
+    row_id = iota((2 * rows, 1), 0)
+    parity = (row_id >= rows).astype(jnp.int32)
+    degree = own_source * stride + 2 * (v * rows + row_id - parity * rows) + parity
+    degrees = degree.astype(F32)
+    ratio = degrees * (degrees + 1.0) / (NTRUNC * NTRUNC)
+    rate_all = jnp.broadcast_to(rates[...], (8, levels))
+    rate_hi, rate_lo = split(rate_all)
+    rate_rest = (rate_all - rate_hi.astype(F32) - rate_lo.astype(F32)).astype(BF16)
+    rate_row = dot_nn(rate_hi, spread) + dot_nn(rate_lo, spread) + dot_nn(rate_rest, spread)
+    damp[...] = 1.0 / (1.0 + rate_row[0:1, :] * ratio)
+
+    def lev_copy(c, k):
+        spec, got = ((spec_a, got_a), (spec_b, got_b))[c]
+        return pltpu.make_async_remote_copy(
+            src_ref=spec.at[k - 1],
+            dst_ref=got.at[v],
+            send_sem=lev_send.at[c, k - 1],
+            recv_sem=lev_recv.at[c, k - 1],
+            device_id={"lev": lax.rem(v + k, lev_count)},
+            device_id_type=MESH_IDS,
+        )
+
+    def legendre(c):
+        first, width, base, length = chunks[c]
+        spec, got = ((spec_a, got_a), (spec_b, got_b))[c]
+        for k in wave_steps:
+            wave_copy(c, k).wait_recv()
+
+        def store_pair(at, north, southern):
+            for p, value in enumerate((north + southern, north - southern)):
+                high, low = split(value)
+                pair_hi[p, :width, at : at + LANES] = high
+                pair_lo[p, :width, at : at + LANES] = low
+
+        half = width // 2
+        for q in range(half_waves // 2):
+            even = 2 * q
+            for e, start in ((even, 0), (even + 1, tiles * LANES + LANES)):
+                for t in range(tiles):
+                    at = slice(base + t * width, base + (t + 1) * width)
+                    store_pair(
+                        q * 2 * lats + start + t * LANES,
+                        arrived[e, at, :],
+                        arrived[wave_count - 1 - e, at, :],
+                    )
+            ends = slice(base + tiles * width, base + tiles * width + half)
+
+            def middle(one, two):
+                a, b = arrived[one, ends, :], arrived[two, ends, :]
+                top = jnp.concatenate([a[:, :HALF_TILE], b[:, :HALF_TILE]], axis=1)
+                low = jnp.concatenate([a[:, HALF_TILE:], b[:, HALF_TILE:]], axis=1)
+                return jnp.concatenate([top, low], axis=0)
+
+            store_pair(
+                q * 2 * lats + tiles * LANES,
+                middle(even, even + 1),
+                middle(wave_count - 1 - even, wave_count - 2 - even),
+            )
+
+        for k in lev_steps + (0,):
+            target = lax.rem(v + k, lev_count)
+            at = pl.ds(pl.multiple_of(target * rows, rows), rows)
+            for p in range(2):
+                l_hi, l_lo = table_hi[p, at, :], table_lo[p, at, :]
+                p_hi, p_lo = pair_hi[p, :width, :], pair_lo[p, :width, :]
+                value = dot_nt(l_hi, p_hi) + dot_nt(l_hi, p_lo) + dot_nt(l_lo, p_hi)
+                if k:
+                    spec[k - 1, p] = value
+                else:
+                    got[v, p] = value
+            if k:
+                lev_copy(c, k).start()
+
+    def project(c):
+        first, width, base, length = chunks[c]
+        got = (got_a, got_b)[c]
+        for k in lev_steps:
+            lev_copy(c, k).wait_recv()
+        total = jnp.zeros((2 * rows, mode_cols), F32)
+        for u in range(lev_count):
+            high, low = split(got[u].reshape(2 * rows, width))
+            at = slice(u * cols + first, u * cols + first + width)
+            total += dot_nn(high, m_hi[at, :]) + dot_nn(high, m_lo[at, :]) + dot_nn(low, m_hi[at, :])
+        return total
+
+    legendre(0)
+    modal[...] = project(0)
+    legendre(1)
+    damped = (modal[...] + project(1)) * damp[...]
+    d_hi, d_lo = split(damped)
+    pieces = []
+    for u in range(lev_count):
+        pieces.append(got_a[u].reshape(2 * rows, chunks[0][1]))
+        pieces.append(got_b[u].reshape(2 * rows, chunks[1][1]))
+    spectra = jnp.concatenate(pieces, axis=1)
+    added = dot_nn(d_hi, g_hi[...]) + dot_nn(d_hi, g_lo[...]) + dot_nn(d_lo, g_hi[...])
+    field_row = lax.div(lax.rem(iota((1, all_cols), 1), group), 2)
+    result = jnp.where(field_row == 1, 0.0, spectra) + added
+    result = jnp.where(degree < NTRUNC, result, 0.0)
+    out[0, 0] = result[:rows]
+    out[0, 1] = result[rows:]
+
+    for c in range(2):
+        for k in wave_steps:
+            wave_copy(c, k).wait_send()
+        for k in lev_steps:
+            lev_copy(c, k).wait_send()
+
+
+def kernel_fits(wave_count, lats, cols, slot_count, half_rows, lat_half, lev_count):
+    head = cols - LAST
+    return (
+        slot_count == 1
+        and wave_count % 4 == 0
+        and lats % LANES == HALF_TILE
+        and lats > LANES
+        and lat_half == lats * wave_count // 2
+        and head > 0
+        and head % 16 == 0
+        and lev_count > 1
+        and half_rows % (16 * lev_count) == 0
+        and half_rows % 32 == 0
+    )
+
+
+def centre_out(count):
+    return tuple(sorted(range(1, count), key=lambda k: (abs(2 * k - count), k)))
+
+
+def on_device(
+    fourier,
+    weights,
+    row_points,
+    slot_map,
+    legendre_lookup,
+    to_modes,
+    from_modes,
+    mode_rates,
+    thermal_response_matrix,
+):
+    wave_count = lax.axis_size("wave")
+    lev_count = lax.axis_size("lev")
+    lats, window, cols = fourier.shape
+    slot_count, _, half_rows, lat_half = legendre_lookup.shape
+    if not kernel_fits(wave_count, lats, cols, slot_count, half_rows, lat_half, lev_count):
+        return on_device_plain(
+            fourier,
+            weights,
+            row_points,
+            slot_map,
+            legendre_lookup,
+            to_modes,
+            from_modes,
+            mode_rates,
+            thermal_response_matrix,
+        )
+    levels = to_modes.shape[0]
+    rows = half_rows // lev_count
+    tiles = lats // LANES
+    chunks = []
+    base = 0
+    first = 0
+    for width in (cols - LAST, LAST):
+        length = tiles * width + width // 2
+        chunks.append((first, width, base, length))
+        first += width
+        base += length
+    widths = (chunks[0][1], chunks[1][1])
+    widest = max(widths)
+    all_cols = cols * lev_count
+    mode_cols = 2 * levels
+    sizes = (wave_count, lev_count, tuple(chunks), centre_out(wave_count), centre_out(lev_count))
+    vmem = pl.BlockSpec(memory_space=pltpu.VMEM)
+    smem = pl.BlockSpec(memory_space=pltpu.SMEM)
+    hbm = pl.BlockSpec(memory_space=pl.ANY)
+    out_shape = (1, 2, rows, all_cols)
+    work = 2 * 3 * 2 * half_rows * lat_half * cols
+    return pl.pallas_call(
+        functools.partial(kernel, sizes),
+        out_shape=jax.ShapeDtypeStruct(out_shape, F32),
+        in_specs=[smem, vmem, vmem, vmem, hbm, vmem, vmem, vmem, vmem],
+        out_specs=vmem,
+        scratch_shapes=[
+            pltpu.VMEM((2, half_rows, lat_half), F32),
+            pltpu.VMEM((2, half_rows, lat_half), BF16),
+            pltpu.VMEM((2, half_rows, lat_half), BF16),
+            pltpu.VMEM((wave_count - 1, base, LANES), F32),
+            pltpu.VMEM((wave_count, base, LANES), F32),
+            pltpu.VMEM((2, widest, lat_half), BF16),
+            pltpu.VMEM((2, widest, lat_half), BF16),
+            pltpu.VMEM((lev_count - 1, 2, rows, widths[0]), F32),
+            pltpu.VMEM((lev_count - 1, 2, rows, widths[1]), F32),
+            pltpu.VMEM((lev_count, 2, rows, widths[0]), F32),
+            pltpu.VMEM((lev_count, 2, rows, widths[1]), F32),
+            pltpu.VMEM((all_cols, mode_cols), BF16),
+            pltpu.VMEM((all_cols, mode_cols), BF16),
+            pltpu.VMEM((mode_cols, all_cols), BF16),
+            pltpu.VMEM((mode_cols, all_cols), BF16),
+            pltpu.VMEM((2 * rows, mode_cols), F32),
+            pltpu.VMEM((2 * rows, mode_cols), F32),
+            pltpu.SemaphoreType.DMA,
+            pltpu.SemaphoreType.DMA((2, wave_count - 1)),
+            pltpu.SemaphoreType.DMA((2, wave_count - 1)),
+            pltpu.SemaphoreType.DMA((2, lev_count - 1)),
+            pltpu.SemaphoreType.DMA((2, lev_count - 1)),
+        ],
+        compiler_params=pltpu.CompilerParams(
+            collective_id=0, has_side_effects=True, vmem_limit_bytes=52 * 2**20
+        ),
+        cost_estimate=pl.CostEstimate(flops=work, bytes_accessed=2**24, transcendentals=0),
+    )(
+        slot_map,
+        weights.reshape(1, lats),
+        row_points.reshape(wave_count, lats),
+        jnp.transpose(fourier, (1, 2, 0)),
+        legendre_lookup[0],
+        to_modes,
+        from_modes,
+        mode_rates.reshape(1, levels),
+        thermal_response_matrix,
+    )
+
+
 def solution(mesh):
     placed = (
         P("wave", None, "lev"),

time: 172 us -> 90.4 us (0.53)
  the two profiles are of different devices: /device:TPU:0 before, /device:TPU:15 now
where the time goes in v1:
time: 90.4 us; the launch traced here: 90.1 us
  Pallas kernels  83.5 us (92%)
  local copies, waits for them, and re-layouts  6.63 us (7%)
    pallas_call x1, Pallas kernels, on_device(): pl.pallas_call(functools.partial(kernel, sizes), out_shape=jax.ShapeDtype...  83.5 us
    unnamed x11, local copies, waits for them, and re-layouts  5.17 us

profile of v1, /device:TPU:15, one launch (start us, length us, event | category | flops | bytes accessed | tf_op | source)
XLA Modules:
  0.0 90.1 jit_solution(3504331657048375391)
XLA Ops:
  0.0 0.7 reshape.9.weights
  0.7 0.8 reshape.10.points
  1.5 0.0 copy-start
  1.5 0.9 %copy-done = f32[136,136]{1,0:T(8,128)S(1)} copy-done((f32[136,136]{1,0:T(8,128)S(1)}, f32[136,136]{1,0:T(8,128)}, u32[]{:S(2)}) %copy-start) | copy-done | bytes 74008
  2.4 0.0 copy-start.1
  2.4 0.9 %copy-done.1 = f32[136,136]{1,0:T(8,128)S(1)} copy-done((f32[136,136]{1,0:T(8,128)S(1)}, f32[136,136]{1,0:T(8,128)}, u32[]{:S(2)}) %copy-start.1) | copy-done | bytes 74008
  3.3 0.0 copy-start.2
  3.3 0.9 %copy-done.2 = f32[136,136]{1,0:T(8,128)S(1)} copy-done((f32[136,136]{1,0:T(8,128)S(1)}, f32[136,136]{1,0:T(8,128)}, u32[]{:S(2)}) %copy-start.2) | copy-done | bytes 74008
  4.2 0.0 copy-start.3
  4.2 0.7 copy-done.3
  4.9 0.0 copy-start.4
  4.9 0.7 copy-done.4
  5.5 83.5 %shard_map.91 = f32[1,2,160,1088]{3,2,1,0:T(8,128)S(1)} custom-call(s32[6]{0:T(128)S(1)} %copy-done.4, f32[1,320]{1,0:T(1,128)S(1)} %reshape.9.weights, s32[8,320]{1,0:T(8,128)S(1)} %reshape.10.points, f32[6,272,320]{2,1,0:T(8,128)} %bitcast.5, f32[2,640,1280]{2,1,0:T(8,128)} %bitcast.4, f32[136,136]{1,0:T(8,128)S(1)} %copy-done, f32[136,136]{1,0:T(8,128)S(1)} %copy-done.1, ...), custom_call_target="tpu_custom_call" | custom-call | flops 2673868800 | bytes 16777216 | tf_op jit(solution)/shard_map/pallas_call | solution.py:472
  89.0 1.1 %copy.11 = f32[1,2,160,1088]{3,2,1,0:T(8,128)} copy(f32[1,2,160,1088]{3,2,1,0:T(8,128)S(1)} %shard_map.91) | data formatting | bytes 2785280
Async XLA Ops:
  1.5 0.9 %copy-start = (f32[136,136]{1,0:T(8,128)S(1)}, f32[136,136]{1,0:T(8,128)}, u32[]{:S(2)}) copy-start(f32[136,136]{1,0:T(8,128)} %to_modes.1) | copy-start | bytes 221956
  2.4 0.9 %copy-start.1 = (f32[136,136]{1,0:T(8,128)S(1)}, f32[136,136]{1,0:T(8,128)}, u32[]{:S(2)}) copy-start(f32[136,136]{1,0:T(8,128)} %from_modes.1) | copy-start | bytes 221956
  3.3 0.9 %copy-start.2 = (f32[136,136]{1,0:T(8,128)S(1)}, f32[136,136]{1,0:T(8,128)}, u32[]{:S(2)}) copy-start(f32[136,136]{1,0:T(8,128)} %thermal.1) | copy-start | bytes 221956
  4.2 0.7 copy-start.3
  4.9 0.7 copy-start.4

commit v2 on v1

--- a/solution.py
+++ b/solution.py
@@ -104,7 +104,7 @@
 BF16 = jnp.bfloat16
 HALF_TILE = 64
 LANES = 128
-LAST = 128
+NARROW = 64
 MESH_IDS = pl.DeviceIdType.MESH
 
 
@@ -131,16 +131,24 @@
 
 def kernel(
     sizes,
-    slot_map,
+    slot_hbm,
     weights,
     points,
-    fourier,
+    fourier_hbm,
     table_hbm,
+    to_hbm,
+    from_hbm,
+    rates_hbm,
+    thermal_hbm,
+    out,
+    slot_map,
+    fourier_a,
+    fourier_b,
+    fourier_c,
     to_modes,
     from_modes,
     rates,
     thermal,
-    out,
     table,
     table_hi,
     table_lo,
@@ -150,14 +158,18 @@
     pair_lo,
     spec_a,
     spec_b,
+    spec_c,
     got_a,
     got_b,
+    got_c,
     m_hi,
     m_lo,
     g_hi,
     g_lo,
     damp,
     modal,
+    small_sem,
+    fourier_sem,
     table_sem,
     wave_send,
     wave_recv,
@@ -165,7 +177,8 @@
     lev_recv,
 ):
     wave_count, lev_count, chunks, wave_steps, lev_steps = sizes
-    window, cols, lats = fourier.shape
+    window, cols, lats = fourier_hbm.shape
+    fouriers = (fourier_a, fourier_b, fourier_c)
     _, half_rows, lat_half = table_hbm.shape
     levels = to_modes.shape[0]
     all_cols = cols * lev_count
@@ -186,6 +199,21 @@
         pl.semaphore_signal(
             barrier, inc=1, device_id={"lev": lax.rem(v + k, lev_count)}, device_id_type=MESH_IDS
         )
+    slot_copy = pltpu.make_async_copy(slot_hbm, slot_map, small_sem.at[0])
+    slot_copy.start()
+    fourier_copies = []
+    for c, (first, width, base, length) in enumerate(chunks):
+        at = slice(first, first + width)
+        fourier_copies.append(
+            pltpu.make_async_copy(fourier_hbm.at[:, at], fouriers[c], fourier_sem.at[c])
+        )
+        fourier_copies[c].start()
+    small_copies = []
+    for n, (there, here) in enumerate(
+        ((to_hbm, to_modes), (from_hbm, from_modes), (rates_hbm, rates), (thermal_hbm, thermal))
+    ):
+        small_copies.append(pltpu.make_async_copy(there, here, small_sem.at[n + 1]))
+        small_copies[n].start()
     table_copy = pltpu.make_async_copy(table_hbm, table, table_sem)
     table_copy.start()
 
@@ -207,11 +235,12 @@
     arrange = one_hot(iota((lats, lats), 0) == place)
     point_row = points[pl.ds(w, 1), :]
     weight_row = weights[...]
-
-    def arranged(slot, first, width, write):
+    slot_copy.wait()
+
+    def arranged(slot, c, width, write):
         source, used = slot_source(slot)
         keep = (2 * stride * source < point_row).astype(F32) * used.astype(F32)
-        block = fourier[source, first : first + width, :] * (weight_row * keep)
+        block = fouriers[c][source] * (weight_row * keep)
         high, low = split(block)
         moved = dot_nn(high, arrange) + dot_nn(low, arrange)
         for t in range(tiles):
@@ -231,21 +260,23 @@
             device_id_type=MESH_IDS,
         )
 
-    pl.semaphore_wait(barrier, len(wave_steps) + len(lev_steps))
     for c, (first, width, base, length) in enumerate(chunks):
+        fourier_copies[c].wait()
         for k in wave_steps:
 
             def put(at, count, value, k=k, base=base):
                 outgoing[k - 1, base + at : base + at + count, :] = value
 
-            arranged(lax.rem(w + k, wave_count), first, width, put)
+            arranged(lax.rem(w + k, wave_count), c, width, put)
+            if c == 0 and k == wave_steps[0]:
+                pl.semaphore_wait(barrier, len(wave_steps) + len(lev_steps))
             wave_copy(c, k).start()
-    for first, width, base, length in chunks:
+    for c, (first, width, base, length) in enumerate(chunks):
 
         def put_own(at, count, value, base=base):
             arrived[w, base + at : base + at + count, :] = value
 
-        arranged(w, first, width, put_own)
+        arranged(w, c, width, put_own)
 
     table_copy.wait()
     step_rows = 32
@@ -258,6 +289,8 @@
             table_hi[p, at, :] = high
             table_lo[p, at, :] = low
 
+    for copy in small_copies:
+        copy.wait()
     part_mask = (
         lax.rem(iota((all_cols, mode_cols), 0), 2) == lax.rem(iota((all_cols, mode_cols), 1), 2)
     ).astype(F32)
@@ -304,7 +337,7 @@
     damp[...] = 1.0 / (1.0 + rate_row[0:1, :] * ratio)
 
     def lev_copy(c, k):
-        spec, got = ((spec_a, got_a), (spec_b, got_b))[c]
+        spec, got = ((spec_a, got_a), (spec_b, got_b), (spec_c, got_c))[c]
         return pltpu.make_async_remote_copy(
             src_ref=spec.at[k - 1],
             dst_ref=got.at[v],
@@ -316,7 +349,7 @@
 
     def legendre(c):
         first, width, base, length = chunks[c]
-        spec, got = ((spec_a, got_a), (spec_b, got_b))[c]
+        spec, got = ((spec_a, got_a), (spec_b, got_b), (spec_c, got_c))[c]
         for k in wave_steps:
             wave_copy(c, k).wait_recv()
 
@@ -354,38 +387,46 @@
         for k in lev_steps + (0,):
             target = lax.rem(v + k, lev_count)
             at = pl.ds(pl.multiple_of(target * rows, rows), rows)
+            values = []
             for p in range(2):
                 l_hi, l_lo = table_hi[p, at, :], table_lo[p, at, :]
                 p_hi, p_lo = pair_hi[p, :width, :], pair_lo[p, :width, :]
-                value = dot_nt(l_hi, p_hi) + dot_nt(l_hi, p_lo) + dot_nt(l_lo, p_hi)
-                if k:
-                    spec[k - 1, p] = value
-                else:
-                    got[v, p] = value
+                values.append(dot_nt(l_hi, p_hi) + dot_nt(l_hi, p_lo) + dot_nt(l_lo, p_hi))
+            value = jnp.concatenate(values, axis=1 if width == NARROW else 0)
+            if k:
+                spec[k - 1] = value
+            else:
+                got[v] = value
             if k:
                 lev_copy(c, k).start()
 
+    def block(c, u):
+        value = (got_a, got_b, got_c)[c][u]
+        if chunks[c][1] == NARROW:
+            value = jnp.concatenate([value[:, :NARROW], value[:, NARROW:]], axis=0)
+        return value
+
     def project(c):
         first, width, base, length = chunks[c]
-        got = (got_a, got_b)[c]
         for k in lev_steps:
             lev_copy(c, k).wait_recv()
         total = jnp.zeros((2 * rows, mode_cols), F32)
         for u in range(lev_count):
-            high, low = split(got[u].reshape(2 * rows, width))
+            high, low = split(block(c, u))
             at = slice(u * cols + first, u * cols + first + width)
             total += dot_nn(high, m_hi[at, :]) + dot_nn(high, m_lo[at, :]) + dot_nn(low, m_hi[at, :])
         return total
 
     legendre(0)
-    modal[...] = project(0)
     legendre(1)
-    damped = (modal[...] + project(1)) * damp[...]
+    modal[...] = project(0) + project(1)
+    legendre(2)
+    damped = (modal[...] + project(2)) * damp[...]
     d_hi, d_lo = split(damped)
     pieces = []
     for u in range(lev_count):
-        pieces.append(got_a[u].reshape(2 * rows, chunks[0][1]))
-        pieces.append(got_b[u].reshape(2 * rows, chunks[1][1]))
+        for c in range(len(chunks)):
+            pieces.append(block(c, u))
     spectra = jnp.concatenate(pieces, axis=1)
     added = dot_nn(d_hi, g_hi[...]) + dot_nn(d_hi, g_lo[...]) + dot_nn(d_lo, g_hi[...])
     field_row = lax.div(lax.rem(iota((1, all_cols), 1), group), 2)
@@ -394,7 +435,7 @@
     out[0, 0] = result[:rows]
     out[0, 1] = result[rows:]
 
-    for c in range(2):
+    for c in range(len(chunks)):
         for k in wave_steps:
             wave_copy(c, k).wait_send()
         for k in lev_steps:
@@ -402,14 +443,14 @@
 
 
 def kernel_fits(wave_count, lats, cols, slot_count, half_rows, lat_half, lev_count):
-    head = cols - LAST
+    head = cols - 2 * NARROW
     return (
         slot_count == 1
         and wave_count % 4 == 0
         and lats % LANES == HALF_TILE
         and lats > LANES
         and lat_half == lats * wave_count // 2
-        and head > 0
+        and head > NARROW
         and head % 16 == 0
         and lev_count > 1
         and half_rows % (16 * lev_count) == 0
@@ -454,27 +495,32 @@
     chunks = []
     base = 0
     first = 0
-    for width in (cols - LAST, LAST):
+    for width in (cols - 2 * NARROW, NARROW, NARROW):
         length = tiles * width + width // 2
         chunks.append((first, width, base, length))
         first += width
         base += length
-    widths = (chunks[0][1], chunks[1][1])
-    widest = max(widths)
+    widest = chunks[0][1]
+    wide, narrow = (2 * rows, widest), (rows, 2 * NARROW)
     all_cols = cols * lev_count
     mode_cols = 2 * levels
     sizes = (wave_count, lev_count, tuple(chunks), centre_out(wave_count), centre_out(lev_count))
     vmem = pl.BlockSpec(memory_space=pltpu.VMEM)
-    smem = pl.BlockSpec(memory_space=pltpu.SMEM)
     hbm = pl.BlockSpec(memory_space=pl.ANY)
     out_shape = (1, 2, rows, all_cols)
     work = 2 * 3 * 2 * half_rows * lat_half * cols
     return pl.pallas_call(
         functools.partial(kernel, sizes),
         out_shape=jax.ShapeDtypeStruct(out_shape, F32),
-        in_specs=[smem, vmem, vmem, vmem, hbm, vmem, vmem, vmem, vmem],
+        in_specs=[hbm, vmem, vmem] + [hbm] * 6,
         out_specs=vmem,
         scratch_shapes=[
+            pltpu.SMEM((window,), jnp.int32),
+            *(pltpu.VMEM((window, chunk[1], lats), F32) for chunk in chunks),
+            pltpu.VMEM((levels, levels), F32),
+            pltpu.VMEM((levels, levels), F32),
+            pltpu.VMEM((1, levels), F32),
+            pltpu.VMEM((levels, levels), F32),
             pltpu.VMEM((2, half_rows, lat_half), F32),
             pltpu.VMEM((2, half_rows, lat_half), BF16),
             pltpu.VMEM((2, half_rows, lat_half), BF16),
@@ -482,24 +528,28 @@
             pltpu.VMEM((wave_count, base, LANES), F32),
             pltpu.VMEM((2, widest, lat_half), BF16),
             pltpu.VMEM((2, widest, lat_half), BF16),
-            pltpu.VMEM((lev_count - 1, 2, rows, widths[0]), F32),
-            pltpu.VMEM((lev_count - 1, 2, rows, widths[1]), F32),
-            pltpu.VMEM((lev_count, 2, rows, widths[0]), F32),
-            pltpu.VMEM((lev_count, 2, rows, widths[1]), F32),
+            pltpu.VMEM((lev_count - 1, *wide), F32),
+            pltpu.VMEM((lev_count - 1, *narrow), F32),
+            pltpu.VMEM((lev_count - 1, *narrow), F32),
+            pltpu.VMEM((lev_count, *wide), F32),
+            pltpu.VMEM((lev_count, *narrow), F32),
+            pltpu.VMEM((lev_count, *narrow), F32),
             pltpu.VMEM((all_cols, mode_cols), BF16),
             pltpu.VMEM((all_cols, mode_cols), BF16),
             pltpu.VMEM((mode_cols, all_cols), BF16),
             pltpu.VMEM((mode_cols, all_cols), BF16),
             pltpu.VMEM((2 * rows, mode_cols), F32),
             pltpu.VMEM((2 * rows, mode_cols), F32),
+            pltpu.SemaphoreType.DMA((5,)),
+            pltpu.SemaphoreType.DMA((len(chunks),)),
             pltpu.SemaphoreType.DMA,
-            pltpu.SemaphoreType.DMA((2, wave_count - 1)),
-            pltpu.SemaphoreType.DMA((2, wave_count - 1)),
-            pltpu.SemaphoreType.DMA((2, lev_count - 1)),
-            pltpu.SemaphoreType.DMA((2, lev_count - 1)),
+            pltpu.SemaphoreType.DMA((len(chunks), wave_count - 1)),
+            pltpu.SemaphoreType.DMA((len(chunks), wave_count - 1)),
+            pltpu.SemaphoreType.DMA((len(chunks), lev_count - 1)),
+            pltpu.SemaphoreType.DMA((len(chunks), lev_count - 1)),
         ],
         compiler_params=pltpu.CompilerParams(
-            collective_id=0, has_side_effects=True, vmem_limit_bytes=52 * 2**20
+            collective_id=0, has_side_effects=True, vmem_limit_bytes=56 * 2**20
         ),
         cost_estimate=pl.CostEstimate(flops=work, bytes_accessed=2**24, transcendentals=0),
     )(

time: 90.4 us -> 89.5 us (0.990)
  local copies, waits for them, and re-layouts: 6.63 us -> 5.22 us
    unnamed x11 -> x1, local copies, waits for them, and re-layouts: 5.17 us -> 2.58 us
where the time goes in v2:
time: 89.5 us; the launch traced here: 89.2 us
  Pallas kernels  84 us (94%)
  local copies, waits for them, and re-layouts  5.22 us (6%)
    pallas_call x1, Pallas kernels, on_device(): pl.pallas_call(functools.partial(kernel, sizes), out_shape=jax.ShapeDtype...  84 us
    unnamed x1, local copies, waits for them, and re-layouts  2.58 us

profile of v2, /device:TPU:15, one launch (start us, length us, event | category | flops | bytes accessed | tf_op | source)
XLA Modules:
  0.0 89.2 jit_solution(8782800627710252396)
XLA Ops:
  0.0 1.3 %reshape.9.weights = f32[1,320]{1,0:T(1,128)} reshape(f32[320]{0:T(512)} %param.10) | data formatting | bytes 2560 | tf_op jit(solution)/shard_map/reshape | solution.py:557
  1.3 1.4 %reshape.10.points = s32[8,320]{1,0:T(8,128)} reshape(s32[2560]{0:T(1024)} %param.11) | data formatting | bytes 20480 | tf_op jit(solution)/shard_map/reshape | solution.py:558
  2.6 84.0 %shard_map.91 = f32[1,2,160,1088]{3,2,1,0:T(8,128)} custom-call(s32[6]{0:T(128)} %slot_hbm.1, f32[1,320]{1,0:T(1,128)} %reshape.9.weights, s32[8,320]{1,0:T(8,128)} %reshape.10.points, f32[6,272,320]{2,1,0:T(8,128)} %bitcast.4, f32[2,640,1280]{2,1,0:T(8,128)} %bitcast.3, f32[136,136]{1,0:T(8,128)} %to_hbm.1, f32[136,136]{1,0:T(8,128)} %from_hbm.1, ...), custom_call_target="tpu_custom_call" | custom-call | flops 2673868800 | bytes 16777216 | tf_op jit(solution)/shard_map/pallas_call | solution.py:512
  86.6 2.6 %copy.11 = f32[1,2,160,1088]{3,2,1,0:T(8,128)} copy(f32[1,2,160,1088]{3,2,1,0:T(8,128)} %shard_map.91) | data formatting | bytes 2785280

commit v3 on v2

--- a/solution.py
+++ b/solution.py
@@ -190,10 +190,18 @@
     w = lax.axis_index("wave")
     v = lax.axis_index("lev")
 
+    side = lax.div(w, half_waves)
+    local = lax.rem(w, half_waves)
+
+    def peer(k):
+        crossing = k <= half_waves
+        there = 1 - side if crossing else side
+        return there * half_waves + lax.rem(local + (k - 1 if crossing else k - half_waves), half_waves)
+
     barrier = pltpu.get_barrier_semaphore()
     for k in wave_steps:
         pl.semaphore_signal(
-            barrier, inc=1, device_id={"wave": lax.rem(w + k, wave_count)}, device_id_type=MESH_IDS
+            barrier, inc=1, device_id={"wave": peer(k)}, device_id_type=MESH_IDS
         )
     for k in lev_steps:
         pl.semaphore_signal(
@@ -256,21 +264,34 @@
             dst_ref=arrived.at[w, pl.ds(base, length)],
             send_sem=wave_send.at[c, k - 1],
             recv_sem=wave_recv.at[c, k - 1],
-            device_id={"wave": lax.rem(w + k, wave_count)},
+            device_id={"wave": peer(k)},
             device_id_type=MESH_IDS,
         )
 
-    for c, (first, width, base, length) in enumerate(chunks):
-        fourier_copies[c].wait()
-        for k in wave_steps:
-
-            def put(at, count, value, k=k, base=base):
-                outgoing[k - 1, base + at : base + at + count, :] = value
-
-            arranged(lax.rem(w + k, wave_count), c, width, put)
-            if c == 0 and k == wave_steps[0]:
-                pl.semaphore_wait(barrier, len(wave_steps) + len(lev_steps))
-            wave_copy(c, k).start()
+    sends = []
+    inner = []
+    for c in range(len(chunks)):
+        for k in wave_steps[:half_waves]:
+            sends.append((c, k))
+            if inner:
+                sends.append(inner.pop(0))
+        sends += inner
+        inner = [(c, k) for k in wave_steps[half_waves:]]
+    sends += inner
+    ready = set()
+    for c, k in sends:
+        first, width, base, length = chunks[c]
+        if c not in ready:
+            fourier_copies[c].wait()
+            ready.add(c)
+
+        def put(at, count, value, k=k, base=base):
+            outgoing[k - 1, base + at : base + at + count, :] = value
+
+        arranged(peer(k), c, width, put)
+        if (c, k) == sends[0]:
+            pl.semaphore_wait(barrier, len(wave_steps) + len(lev_steps))
+        wave_copy(c, k).start()
     for c, (first, width, base, length) in enumerate(chunks):
 
         def put_own(at, count, value, base=base):
@@ -504,7 +525,7 @@
     wide, narrow = (2 * rows, widest), (rows, 2 * NARROW)
     all_cols = cols * lev_count
     mode_cols = 2 * levels
-    sizes = (wave_count, lev_count, tuple(chunks), centre_out(wave_count), centre_out(lev_count))
+    sizes = (wave_count, lev_count, tuple(chunks), tuple(range(1, wave_count)), centre_out(lev_count))
     vmem = pl.BlockSpec(memory_space=pltpu.VMEM)
     hbm = pl.BlockSpec(memory_space=pl.ANY)
     out_shape = (1, 2, rows, all_cols)

time: 89.5 us -> 92.2 us (1.030); the launches traced: 89.2 us -> 90.4 us
  Pallas kernels: 84 us -> 85.2 us
    pallas_call x1, Pallas kernels: 84 us -> 85.2 us  [on_device(): pl.pallas_call(functools.partial(kernel, sizes), out_shape=jax.ShapeDtype...]
where the time goes in v3:
time: 92.2 us; the launch traced here: 90.4 us
  Pallas kernels  85.2 us (92%)
  local copies, waits for them, and re-layouts  5.22 us (6%)
    pallas_call x1, Pallas kernels, on_device(): pl.pallas_call(functools.partial(kernel, sizes), out_shape=jax.ShapeDtype...  85.2 us
    unnamed x1, local copies, waits for them, and re-layouts  2.58 us

profile of v3, /device:TPU:15, one launch (start us, length us, event | category | flops | bytes accessed | tf_op | source)
XLA Modules:
  0.0 90.4 jit_solution(13944181061238877846)
XLA Ops:
  0.0 1.3 %reshape.9.weights = f32[1,320]{1,0:T(1,128)} reshape(f32[320]{0:T(512)} %param.10) | data formatting | bytes 2560 | tf_op jit(solution)/shard_map/reshape | solution.py:578
  1.3 1.4 %reshape.10.points = s32[8,320]{1,0:T(8,128)} reshape(s32[2560]{0:T(1024)} %param.11) | data formatting | bytes 20480 | tf_op jit(solution)/shard_map/reshape | solution.py:579
  2.6 85.2 %shard_map.91 = f32[1,2,160,1088]{3,2,1,0:T(8,128)} custom-call(s32[6]{0:T(128)} %slot_hbm.1, f32[1,320]{1,0:T(1,128)} %reshape.9.weights, s32[8,320]{1,0:T(8,128)} %reshape.10.points, f32[6,272,320]{2,1,0:T(8,128)} %bitcast.4, f32[2,640,1280]{2,1,0:T(8,128)} %bitcast.3, f32[136,136]{1,0:T(8,128)} %to_hbm.1, f32[136,136]{1,0:T(8,128)} %from_hbm.1, ...), custom_call_target="tpu_custom_call" | custom-call | flops 2673868800 | bytes 16777216 | tf_op jit(solution)/shard_map/pallas_call | solution.py:533
  87.8 2.6 %copy.11 = f32[1,2,160,1088]{3,2,1,0:T(8,128)} copy(f32[1,2,160,1088]{3,2,1,0:T(8,128)} %shard_map.91) | data formatting | bytes 2785280

commit v4 on v2

--- a/solution.py
+++ b/solution.py
@@ -459,7 +459,7 @@
 
 
 def centre_out(count):
-    return tuple(sorted(range(1, count), key=lambda k: (abs(2 * k - count), k)))
+    return tuple(sorted(range(1, count), key=lambda k: (-abs(2 * k - count), k)))
 
 
 def on_device(

time: 89.5 us -> 91.4 us (1.021)
  the two profiles are of different devices: /device:TPU:15 before, /device:TPU:4 now
where the time goes in v4:
time: 91.4 us; the launch traced here: 91.1 us
  Pallas kernels  85.8 us (94%)
  local copies, waits for them, and re-layouts  5.22 us (6%)
    pallas_call x1, Pallas kernels, on_device(): pl.pallas_call(functools.partial(kernel, sizes), out_shape=jax.ShapeDtype...  85.8 us
    unnamed x1, local copies, waits for them, and re-layouts  2.58 us

profile of v4, /device:TPU:4, one launch (start us, length us, event | category | flops | bytes accessed | tf_op | source)
XLA Modules:
  0.0 91.1 jit_solution(16536171962336180810)
XLA Ops:
  0.0 1.3 %reshape.9.weights = f32[1,320]{1,0:T(1,128)} reshape(f32[320]{0:T(512)} %param.10) | data formatting | bytes 2560 | tf_op jit(solution)/shard_map/reshape | solution.py:557
  1.3 1.4 %reshape.10.points = s32[8,320]{1,0:T(8,128)} reshape(s32[2560]{0:T(1024)} %param.11) | data formatting | bytes 20480 | tf_op jit(solution)/shard_map/reshape | solution.py:558
  2.6 85.8 %shard_map.91 = f32[1,2,160,1088]{3,2,1,0:T(8,128)} custom-call(s32[6]{0:T(128)} %slot_hbm.1, f32[1,320]{1,0:T(1,128)} %reshape.9.weights, s32[8,320]{1,0:T(8,128)} %reshape.10.points, f32[6,272,320]{2,1,0:T(8,128)} %bitcast.4, f32[2,640,1280]{2,1,0:T(8,128)} %bitcast.3, f32[136,136]{1,0:T(8,128)} %to_hbm.1, f32[136,136]{1,0:T(8,128)} %from_hbm.1, ...), custom_call_target="tpu_custom_call" | custom-call | flops 2673868800 | bytes 16777216 | tf_op jit(solution)/shard_map/pallas_call | solution.py:512
  88.5 2.6 %copy.11 = f32[1,2,160,1088]{3,2,1,0:T(8,128)} copy(f32[1,2,160,1088]{3,2,1,0:T(8,128)} %shard_map.91) | data formatting | bytes 2785280
